TPU v7x, 32 devices: a whole 2x2x4 slice. The times are simulated.
32 devices in a mesh: seq: 16 (over z, x, core), head: 2 (over y).
Axes of the slice: x: 2, y: 2, z: 4, core: 2. Of those that a mesh axis runs over, the one named last changes fastest.
Arguments:
- queries: bfloat16 [6, 16, 128, 3072], P(None, None, 'seq', 'head'), may hold values from -6 to 6
- key_field: bfloat16 [6, 16, 128, 3072], P(None, None, 'seq', 'head'), may hold values from -6 to 6
- value_field: bfloat16 [6, 16, 128, 3072], P(None, None, 'seq', 'head'), may hold values from -6 to 6
Outputs:
- attended: bfloat16 [6, 16, 128, 3072], P(None, 'head', 'seq')
All inputs are finite; a program needn't handle non-finite values.
Results may differ from a plain program's by a relative error of at most 0.0047.
Values may be sent and summed in bfloat16 or wider, within the bound.
A program may use at most 256 MiB of HBM per device.

v0:
```python
import jax
import jax.numpy as jnp
from jax import lax
from jax.sharding import PartitionSpec as P

HD = 128
TF = 6
TH = 8


def padded(cells, sides, width):
    for axis, dim in sides:
        count = lax.axis_size(axis)
        ends = count - 1
        head = lax.slice_in_dim(cells, 0, width, axis=dim)
        tail = lax.slice_in_dim(cells, cells.shape[dim] - width, cells.shape[dim], axis=dim)
        cells = jnp.concatenate(
            [
                lax.ppermute(tail, axis, [(i, (i + 1) % count) for i in range(ends)]),
                cells,
                lax.ppermute(head, axis, [((i + 1) % count, i) for i in range(ends)]),
            ],
            axis=dim,
        )
    return cells


def attend_tile(query_rows, key_rows, value_rows, allowed):
    head_count = query_rows.shape[1] // HD
    query_heads = query_rows.reshape(query_rows.shape[0], head_count, HD)
    key_heads = key_rows.reshape(key_rows.shape[0], head_count, HD)
    value_heads = value_rows.reshape(value_rows.shape[0], head_count, HD)
    scores = jnp.einsum(
        "qhd,khd->hqk", query_heads, key_heads, preferred_element_type=jnp.float32
    ) * HD ** (-0.5)
    scores = jnp.where(allowed[None, None, :], scores, -jnp.inf)
    row_max = jnp.max(scores, axis=2, keepdims=True)
    weights = jnp.exp(scores - row_max)
    weight_sum = jnp.sum(weights, axis=2, keepdims=True)
    probabilities = weights.astype(jnp.bfloat16)
    combined = jnp.einsum(
        "hqk,khd->qhd", probabilities, value_heads, preferred_element_type=jnp.float32
    )
    combined = combined / jnp.transpose(weight_sum, (1, 0, 2))
    return combined.reshape(query_rows.shape[0], -1).astype(jnp.bfloat16)


def on_device(queries, key_field, value_field):
    frame_count, row_count, col_count, feat_count = queries.shape
    frame_tiles = frame_count // TF
    row_tiles = row_count // TH
    device_count = lax.axis_size("seq")
    position = lax.axis_index("seq")
    stacked = jnp.stack([key_field, value_field])
    window = padded(stacked, (("seq", 3),), col_count)
    side_index = jnp.arange(3 * col_count, dtype=jnp.int32) // col_count
    lower_ok = position > 0
    upper_ok = position < device_count - 1
    col_ok = jnp.where(side_index == 0, lower_ok, jnp.where(side_index == 2, upper_ok, True))
    f_low = max(0, 0 - 1) * TF
    f_high = min(frame_tiles, 2) * TF
    row_pieces = []
    for row_tile in range(row_tiles):
        h_low = max(0, row_tile - 1) * TH
        h_high = min(row_tiles, row_tile + 2) * TH
        allowed = jnp.broadcast_to(
            col_ok[None, None, :], (f_high - f_low, h_high - h_low, 3 * col_count)
        ).reshape(-1)
        block = window.reshape(2, -1, feat_count)
        query_rows = queries[0:TF, row_tile * TH : (row_tile + 1) * TH].reshape(-1, feat_count)
        result = attend_tile(query_rows, block[0], block[1], allowed)
        row_pieces.append(result.reshape(TF, TH, col_count, feat_count))
    result = jnp.concatenate(row_pieces, 1)
    attended = result
    attended = lax.all_to_all(attended, "head", split_axis=1, concat_axis=3, tiled=True)
    return attended


def solution(mesh):
    in_specs = (
        P(None, None, "seq", "head"),
        P(None, None, "seq", "head"),
        P(None, None, "seq", "head"),
    )
    out_specs = P(None, "head", "seq", None)
    return jax.shard_map(
        on_device, mesh=mesh, in_specs=in_specs, out_specs=out_specs, check_vma=False
    )
```

profile of v0, /device:TPU:2, one launch (start us, length us, event | category | flops | bytes accessed | tf_op | source)
XLA Modules:
  0.0 309.5 jit_solution(6326172517950696718)
XLA Ops:
  0.0 0.0 copy-start
  0.0 5.1 %pad_maximum_fusion.1 = bf16[2,6,16,8,1536]{4,3,2,1,0:T(8,128)(2,1)} fusion(bf16[1,6,16,8,1536]{4,3,2,1,0:T(8,128)(2,1)} %bitcast.58, bf16[1,6,16,8,1536]{4,3,2,1,0:T(8,128)(2,1)} %bitcast.60), kind=kLoop, calls=%fused_computation.21 | loop fusion | flops 2359296 | bytes 9437184 | tf_op jit(solution)/shard_map/stack | solution.py:54
  5.1 1.9 collective-permute-start.1
  7.0 2.4 collective-permute-start
  9.5 0.1 broadcast_in_dim.52
  9.6 2.9 fusion.29
  12.4 3.4 %reshape_reshape.6 = bf16[384,12,128]{2,1,0:T(8,128)(2,1)} reshape(bf16[6,8,8,1536]{3,2,1,0:T(8,128)(2,1)} %get-tuple-element.9) | data formatting | bytes 2359296 | tf_op jit(solution)/shard_map/reshape;reshape | solution.py:30
  15.9 1.8 reshape_reshape.7
  17.6 41.3 %collective-permute-done.1 = bf16[2,6,16,8,1536]{4,3,2,1,0:T(8,128)(2,1)} collective-permute-done((bf16[2,6,16,8,1536]{4,3,2,1,0:T(8,128)(2,1)}, bf16[2,6,16,8,1536]{4,3,2,1,0:T(8,128)(2,1)}, u32[]{:S(2)}, u32[]{:S(2)}) %collective-permute-start.1) | collective-permute-done | bytes 4718624 | tf_op jit(solution)/shard_map/ppermute | solution.py:21
  58.9 53.4 %collective-permute-done = bf16[2,6,16,8,1536]{4,3,2,1,0:T(8,128)(2,1)} collective-permute-done((bf16[2,6,16,8,1536]{4,3,2,1,0:T(8,128)(2,1)}, bf16[2,6,16,8,1536]{4,3,2,1,0:T(8,128)(2,1)}, u32[]{:S(2)}, u32[]{:S(2)}) %collective-permute-start) | collective-permute-done | bytes 4718624 | tf_op jit(solution)/shard_map/ppermute | solution.py:19
  112.3 0.0 copy-done
  112.3 5.3 %pad_maximum_fusion = bf16[2,6,16,24,1536]{4,3,2,1,0:T(8,128)(2,1)S(1)} fusion(bf16[2,6,16,8,1536]{4,3,2,1,0:T(8,128)(2,1)} %collective-permute-done.1, bf16[1,6,16,8,1536]{4,3,2,1,0:T(8,128)(2,1)S(1)} %bitcast.59, bf16[1,6,16,8,1536]{4,3,2,1,0:T(8,128)(2,1)} %bitcast.61, bf16[2,6,16,8,1536]{4,3,2,1,0:T(8,128)(2,1)} %collective-permute-done), kind=kLoop, calls=%fused_computation.16 | loop fusion | flops 56623104 | bytes 28311552 | tf_op jit(solution)/shard_map/concatenate | solution.py:17
  117.7 5.3 %fusion.28 = (bf16[1,6,16,24,1536]{4,3,2,1,0:T(8,128)(2,1)}, bf16[1,6,16,24,1536]{4,3,2,1,0:T(8,128)(2,1)}) fusion(bf16[2,6,16,24,1536]{4,3,2,1,0:T(8,128)(2,1)S(1)} %pad_maximum_fusion), kind=kLoop, calls=%fused_computation.38 | loop fusion | bytes 28311552 | tf_op jit(solution)/shard_map/slice | solution.py:71
  123.0 13.6 %reshape_squeeze.9 = bf16[2304,12,128]{2,1,0:T(8,128)(2,1)} reshape(bf16[1,6,16,24,1536]{4,3,2,1,0:T(8,128)(2,1)} %get-tuple-element.7) | data formatting | bytes 14155776 | tf_op jit(solution)/shard_map/reshape;squeeze | solution.py:31
  136.6 13.7 %reshape_squeeze.8 = bf16[2304,12,128]{2,1,0:T(8,128)(2,1)} reshape(bf16[1,6,16,24,1536]{4,3,2,1,0:T(8,128)(2,1)} %get-tuple-element.8) | data formatting | bytes 14155776 | tf_op jit(solution)/shard_map/reshape;squeeze | solution.py:32
  150.3 0.0 copy-start.3
  150.3 12.4 %copy.21 = bf16[2304,12,128]{0,2,1:T(8,128)(2,1)} copy(bf16[2304,12,128]{2,1,0:T(8,128)(2,1)} %reshape_squeeze.8) | data formatting | bytes 14155776 | tf_op jit(solution)/shard_map/reshape;squeeze | solution.py:32
  162.7 0.0 copy-done.3
  162.7 0.0 copy-start.2
  162.7 21.0 %bitcast_reduce_fusion.1 = (f32[12,384]{1,0:T(8,128)S(1)}, f32[12,2304,384]{2,1,0:T(8,128)}) fusion(pred[2304]{0:T(1024)(128)(4,1)S(1)} %broadcast_in_dim.52, bf16[384,12,128]{2,1,0:T(8,128)(2,1)S(1)} %copy-done.3, bf16[2304,12,128]{2,1,0:T(8,128)(2,1)} %reshape_squeeze.9), kind=kOutput, calls=%fused_computation.4 | convolution fusion | flops 2749754880 | bytes 50745600 | tf_op jit(solution)/shard_map/qhd,khd->hqk/dot_general | solution.py:33
  183.7 0.0 copy-done.2
  183.7 39.6 %fusion.2 = (f32[12,384]{1,0:T(8,128)S(1)}, f32[12,384]{1,0:T(8,128)S(1)}, f32[12,2304,384]{2,1,0:T(8,128)}) fusion(f32[12,2304,384]{2,1,0:T(8,128)} %get-tuple-element.12, f32[12,384]{1,0:T(8,128)S(1)} %get-tuple-element.11, pred[2304]{0:T(1024)(128)(4,1)S(1)} %broadcast_in_dim.52, bf16[384,12,128]{2,1,0:T(8,128)(2,1)S(1)} %copy-done.2, ...), kind=kOutput, calls=%fused_computation.8 | convolution fusion | flops 2792217600 | bytes 93249792 | tf_op jit(solution)/shard_map/qhd,khd->hqk/dot_general | solution.py:33
  223.3 20.8 %fusion.17 = bf16[384,12,128]{0,2,1:T(8,128)(2,1)} fusion(bf16[2304,12,128]{0,2,1:T(8,128)(2,1)} %copy.21, f32[12,2304,384]{2,1,0:T(8,128)} %get-tuple-element.12, f32[12,384]{1,0:T(8,128)S(1)} %get-tuple-element.11, pred[2304]{0:T(1024)(128)(4,1)S(1)} %broadcast_in_dim.52, f32[384,12]{0,1:T(8,128)S(1)} %bitcast.64), kind=kOutput, calls=%fused_computation.26 | convolution fusion | flops 2761555968 | bytes 50764032 | tf_op jit(solution)/shard_map/hqk,khd->qhd/dot_general | solution.py:41
  244.1 0.0 copy-start.1
  244.1 18.3 %fusion.4 = f32[12,384]{1,0:T(8,128)S(1)} fusion(f32[12,2304,384]{2,1,0:T(8,128)} %get-tuple-element.13, f32[12,384]{1,0:T(8,128)S(1)} %get-tuple-element.6, pred[2304]{0:T(1024)(128)(4,1)S(1)} %broadcast_in_dim.52), kind=kLoop, calls=%fused_computation.10 | loop fusion | flops 42462720 | bytes 42506496 | tf_op jit(solution)/shard_map/reduce_sum | solution.py:39
  262.4 0.0 copy-done.1
  262.4 18.5 %fusion.16 = bf16[384,12,128]{0,2,1:T(8,128)(2,1)S(1)} fusion(bf16[2304,12,128]{0,2,1:T(8,128)(2,1)S(1)} %copy-done.1, f32[12,2304,384]{2,1,0:T(8,128)} %get-tuple-element.13, f32[12,384]{1,0:T(8,128)S(1)} %get-tuple-element.6, pred[2304]{0:T(1024)(128)(4,1)S(1)} %broadcast_in_dim.52, f32[384,12]{0,1:T(8,128)S(1)} %bitcast.63), kind=kOutput, calls=%fused_computation.24 | convolution fusion | flops 2761555968 | bytes 50764032 | tf_op jit(solution)/shard_map/hqk,khd->qhd/dot_general | solution.py:41
  280.9 1.4 copy.28
  282.3 0.8 convert_element_type.25
  283.2 2.3 copy.23
  285.5 1.6 convert_element_type.22
  287.1 1.5 pad_maximum_fusion.2
  288.6 0.2 copy.29
  288.8 19.0 %all_to_all.18 = bf16[6,16,8,1536]{3,2,0,1:T(8,128)(2,1)S(1)} all-to-all(bf16[6,16,8,1536]{3,2,0,1:T(8,128)(2,1)S(1)} %copy.29), channel_id=1, replica_groups=mesh['seq'=16,'head'=2] {'head'}, dimensions={1} | all-to-all | bytes 4718592 | tf_op jit(solution)/shard_map/all_to_all | solution.py:75
  307.8 1.7 copy.30
  (2 shorter events, 0.0 us)
Async XLA Ops:
  0.0 112.3 %copy-start = (bf16[6,16,8,1536]{3,2,1,0:T(8,128)(2,1)S(1)}, bf16[6,16,8,1536]{3,2,1,0:T(8,128)(2,1)}, u32[]{:S(2)}) copy-start(bf16[6,16,8,1536]{3,2,1,0:T(8,128)(2,1)} %param.5) | copy-start | bytes 7077892
  5.1 53.9 %collective-permute-start.1 = (bf16[2,6,16,8,1536]{4,3,2,1,0:T(8,128)(2,1)}, bf16[2,6,16,8,1536]{4,3,2,1,0:T(8,128)(2,1)}, u32[]{:S(2)}, u32[]{:S(2)}) collective-permute-start(bf16[2,6,16,8,1536]{4,3,2,1,0:T(8,128)(2,1)} %pad_maximum_fusion.1), channel_id=1, source_target_pairs={{2,0},{4,2},{6,4},{8,6},{10,8},{12,10},{14,12},{16,14},{18,16},{20... | collective-permute-start | bytes 14155784 | tf_op jit(solution)/shard_map/ppermute | solution.py:21
  7.0 105.3 %collective-permute-start = (bf16[2,6,16,8,1536]{4,3,2,1,0:T(8,128)(2,1)}, bf16[2,6,16,8,1536]{4,3,2,1,0:T(8,128)(2,1)}, u32[]{:S(2)}, u32[]{:S(2)}) collective-permute-start(bf16[2,6,16,8,1536]{4,3,2,1,0:T(8,128)(2,1)} %pad_maximum_fusion.1), channel_id=1, source_target_pairs={{0,2},{2,4},{4,6},{6,8},{8,10},{10,12},{12,14},{14,16},{16,18},{18... | collective-permute-start | bytes 14155784 | tf_op jit(solution)/shard_map/ppermute | solution.py:19
  150.3 12.4 %copy-start.3 = (bf16[384,12,128]{2,1,0:T(8,128)(2,1)S(1)}, bf16[384,12,128]{2,1,0:T(8,128)(2,1)}, u32[]{:S(2)}) copy-start(bf16[384,12,128]{2,1,0:T(8,128)(2,1)} %reshape_reshape.6) | copy-start | bytes 3538948
  162.7 21.0 %copy-start.2 = (bf16[384,12,128]{2,1,0:T(8,128)(2,1)S(1)}, bf16[384,12,128]{2,1,0:T(8,128)(2,1)}, u32[]{:S(2)}) copy-start(bf16[384,12,128]{2,1,0:T(8,128)(2,1)} %reshape_reshape.7) | copy-start | bytes 3538948
  244.1 18.3 %copy-start.1 = (bf16[2304,12,128]{0,2,1:T(8,128)(2,1)S(1)}, bf16[2304,12,128]{0,2,1:T(8,128)(2,1)}, u32[]{:S(2)}) copy-start(bf16[2304,12,128]{0,2,1:T(8,128)(2,1)} %copy.21) | copy-start | bytes 21233668
where the time goes:
time: 311 us; the launch traced here: 310 us
  matrix products  99.9 us (32%)
  waiting for transfers between devices  94.7 us (30%)
  local copies, waits for them, and re-layouts  61.3 us (20%)
  other arithmetic  30.2 us (10%)
  blocking collectives  19 us (6%)
  starting transfers between devices  4.32 us (1%)
    dot_general x2, matrix products, attend_tile(): jnp.einsum('qhd,khd->hqk', query_heads, key_heads, preferred_element_type...  60.6 us
    ppermute x1, waiting for transfers between devices, padded(): lax.ppermute(tail, axis, [(i, (i + 1) % count) for i in range(ends)])  53.4 us
    ppermute x1, waiting for transfers between devices, padded(): lax.ppermute(head, axis, [((i + 1) % count, i) for i in range(ends)])  41.3 us
    dot_general x2, matrix products, attend_tile(): jnp.einsum('hqk,khd->qhd', probabilities, value_heads, preferred_element_...  39.3 us
    another operation x2, local copies, waits for them, and re-layouts, attend_tile(): value_heads = value_rows.reshape(value_rows.shape[0], head_count, HD)  26.1 us
    all_to_all x1, blocking collectives, on_device(): lax.all_to_all(attended, 'head', split_axis=1, concat_axis=3, tiled=True)  19 us
    reduce_sum x1, other arithmetic, attend_tile(): weight_sum = jnp.sum(weights, axis=2, keepdims=True)  18.3 us
    another operation x1, local copies, waits for them, and re-layouts, attend_tile(): key_heads = key_rows.reshape(key_rows.shape[0], head_count, HD)  13.6 us
  transfers between devices with their start and end apart: 2, of which 2 were waited for; matrix products, arithmetic and copies ran while one was open for 3% of the time, Pallas kernels for 0%

commit v1 on v0

v1 whole, which is shorter than its diff:
```python
import functools

import jax
import jax.numpy as jnp
from jax import lax
from jax.experimental import pallas as pl
from jax.experimental.pallas import tpu as pltpu
from jax.sharding import PartitionSpec as P

HD = 128
AHEAD = 3
MISSING = 1e30
LOG2E = 1.4426950408889634


def kernel(q_ref, k_ref, v_ref, out_ref, q_buf, kv_buf, o_buf,
           load_sem, send_sem, recv_sem, own_sem, osend_sem, orecv_sem, *, seq, head):
    heads = q_buf.shape[0]
    tokens = q_buf.shape[1]
    frames = o_buf.shape[1]
    rows = out_ref.shape[1]
    me = lax.axis_index("seq")
    part = lax.axis_index("head")
    has_left = me > 0
    has_right = me < seq - 1

    def columns(j):
        return pl.ds(pl.multiple_of(j * HD, HD), HD)

    def loads(h):
        return (
            pltpu.make_async_copy(k_ref.at[:, columns(h)], kv_buf.at[1, h, 0], load_sem.at[0, h]),
            pltpu.make_async_copy(v_ref.at[:, columns(h)], kv_buf.at[1, h, 1], load_sem.at[1, h]),
            pltpu.make_async_copy(q_ref.at[:, columns(h)], q_buf.at[h], load_sem.at[2, h]),
        )

    def to_side(h, side):
        target = me + 1 if side == 0 else me - 1
        return pltpu.make_async_remote_copy(
            src_ref=kv_buf.at[1, h],
            dst_ref=kv_buf.at[0 if side == 0 else 2, h],
            send_sem=send_sem.at[side, h],
            recv_sem=recv_sem.at[side, h],
            device_id={"seq": target},
            device_id_type=pl.DeviceIdType.MESH,
        )

    def out_slices(h, p, sender):
        src = o_buf.at[h, :, pl.ds(pl.multiple_of(p * rows, 16), rows), :]
        dst = out_ref.at[:, :, columns(sender * heads + h)]
        return src, dst

    def to_part(h, step):
        p = lax.rem(part + step, head)
        src, dst = out_slices(h, p, part)
        return pltpu.make_async_remote_copy(
            src_ref=src,
            dst_ref=dst,
            send_sem=osend_sem.at[step, h],
            recv_sem=orecv_sem.at[step, h],
            device_id={"head": p},
            device_id_type=pl.DeviceIdType.MESH,
        )

    def to_self(h):
        src, dst = out_slices(h, part, part)
        return pltpu.make_async_copy(src, dst, own_sem.at[h])

    def start_loads(h, carry):
        for copy in loads(h):
            copy.start()
        return carry

    lax.fori_loop(0, heads, start_loads, 0)

    barrier = pltpu.get_barrier_semaphore()
    for near in (lax.rem(me + 1, seq), lax.rem(me + seq - 1, seq)):
        pl.semaphore_signal(barrier, inc=1, device_id={"seq": near}, device_id_type=pl.DeviceIdType.MESH)
    for step in range(1, head):
        pl.semaphore_signal(barrier, inc=1, device_id={"head": lax.rem(part + step, head)},
                            device_id_type=pl.DeviceIdType.MESH)
    pl.semaphore_wait(barrier, 2 + head - 1)

    def send(h):
        for copy in loads(h):
            copy.wait()

        @pl.when(has_right)
        def _():
            to_side(h, 0).start()

        @pl.when(has_left)
        def _():
            to_side(h, 1).start()

    ahead = min(AHEAD, heads)

    def first_sends(h, carry):
        send(h)
        return carry

    lax.fori_loop(0, ahead, first_sends, 0)

    @pl.when(jnp.logical_not(has_left))
    def _():
        kv_buf[0] = jnp.zeros_like(kv_buf[0])

    @pl.when(jnp.logical_not(has_right))
    def _():
        kv_buf[2] = jnp.zeros_like(kv_buf[2])

    shift = (
        jnp.where(has_left, 0.0, MISSING).astype(jnp.float32),
        jnp.float32(0.0),
        jnp.where(has_right, 0.0, MISSING).astype(jnp.float32),
    )
    chunk = 256 if tokens % 256 == 0 else tokens
    factor = HD ** -0.5 * LOG2E
    per_frame = tokens // frames

    def attend(h):
        def rows_of(c, carry):
            at = pl.ds(pl.multiple_of(c * chunk, chunk), chunk)
            q = q_buf[h, at, :]
            scores = [
                lax.dot_general(q, kv_buf[b, h, 0], (((1,), (1,)), ((), ())),
                                preferred_element_type=jnp.float32)
                for b in range(3)
            ]
            tops = [jnp.max(s, axis=1, keepdims=True) - shift[b] for b, s in enumerate(scores)]
            top = jnp.maximum(jnp.maximum(tops[0], tops[1]), tops[2])
            total = 0.0
            weight_sum = 0.0
            for b in range(3):
                w = jnp.exp2(scores[b] * factor - (top + shift[b]) * factor)
                weight_sum = weight_sum + jnp.sum(w, axis=1, keepdims=True)
                total = total + jnp.dot(w.astype(jnp.bfloat16), kv_buf[b, h, 1],
                                        preferred_element_type=jnp.float32)
            result = (total / weight_sum).astype(jnp.bfloat16)
            o_buf[h, pl.ds(c * (chunk // per_frame), chunk // per_frame)] = result.reshape(
                chunk // per_frame, per_frame, HD)
            return carry

        lax.fori_loop(0, tokens // chunk, rows_of, 0)

    def step_of(h, carry):
        @pl.when(h + ahead < heads)
        def _():
            send(h + ahead)

        @pl.when(has_left)
        def _():
            to_side(h, 0).wait_recv()

        @pl.when(has_right)
        def _():
            to_side(h, 1).wait_recv()

        attend(h)
        to_self(h).start()
        for step in range(1, head):
            to_part(h, step).start()
        return carry

    lax.fori_loop(0, heads, step_of, 0)

    def finish(h, carry):
        @pl.when(has_right)
        def _():
            to_side(h, 0).wait_send()

        @pl.when(has_left)
        def _():
            to_side(h, 1).wait_send()

        to_self(h).wait()
        for step in range(1, head):
            to_part(h, step).wait_send()
            to_part(h, step).wait_recv()
        return carry

    lax.fori_loop(0, heads, finish, 0)


def on_device(queries, key_field, value_field):
    frames, height, width, feat = queries.shape
    seq = lax.axis_size("seq")
    head = lax.axis_size("head")
    heads = feat // HD
    tokens = frames * height * width
    rows = height // head * width
    result = pl.pallas_call(
        functools.partial(kernel, seq=seq, head=head),
        out_shape=jax.ShapeDtypeStruct((frames, rows, feat * head), jnp.bfloat16),
        in_specs=[pl.BlockSpec(memory_space=pl.ANY)] * 3,
        out_specs=pl.BlockSpec(memory_space=pl.ANY),
        scratch_shapes=[
            pltpu.VMEM((heads, tokens, HD), jnp.bfloat16),
            pltpu.VMEM((3, heads, 2, tokens, HD), jnp.bfloat16),
            pltpu.VMEM((heads, frames, height * width, HD), jnp.bfloat16),
            pltpu.SemaphoreType.DMA((3, heads)),
            pltpu.SemaphoreType.DMA((2, heads)),
            pltpu.SemaphoreType.DMA((2, heads)),
            pltpu.SemaphoreType.DMA((heads,)),
            pltpu.SemaphoreType.DMA((head, heads)),
            pltpu.SemaphoreType.DMA((head, heads)),
        ],
        compiler_params=pltpu.CompilerParams(
            collective_id=0, has_side_effects=True, vmem_limit_bytes=56 * 2 ** 20
        ),
        cost_estimate=pl.CostEstimate(
            flops=12 * heads * tokens * tokens * HD,
            bytes_accessed=8 * tokens * feat,
            transcendentals=3 * heads * tokens * tokens,
        ),
        name="tile_attention",
    )(
        queries.reshape(tokens, feat),
        key_field.reshape(tokens, feat),
        value_field.reshape(tokens, feat),
    )
    return result.reshape(frames, height // head, width, feat * head)


def solution(mesh):
    spec = P(None, None, "seq", "head")
    return jax.shard_map(
        on_device, mesh=mesh, in_specs=(spec, spec, spec),
        out_specs=P(None, "head", "seq", None), check_vma=False,
    )
```

time: 311 us -> 117 us (0.38)
  Pallas kernels: 0 us -> 114 us
  matrix products: 99.9 us -> 0 us
  waiting for transfers between devices: 94.7 us -> 0 us
  local copies, waits for them, and re-layouts: 61.3 us -> 3.32 us
  other arithmetic: 30.2 us -> 0 us
  blocking collectives: 19 us -> 0 us
  starting transfers between devices: 4.32 us -> 0 us
    pallas_call x0 -> x1, Pallas kernels: none -> 114 us  [on_device(): pl.pallas_call(functools.partial(kernel, seq=seq, head=head), out_shape=j...]
    dot_general x4 -> x0, matrix products: 99.9 us -> none  [the longest x2 60.6 us: attend_tile(): jnp.einsum('qhd,khd->hqk', query_heads, key_heads, preferred_element_type...]
    ppermute x2 -> x0, waiting for transfers between devices: 94.7 us -> none  [the longest x1 53.4 us: padded(): lax.ppermute(tail, axis, [(i, (i + 1) % count) for i in range(ends)])]
    another operation x5 -> x0, local copies, waits for them, and re-layouts: 44.9 us -> none  [the longest x2 26.1 us: attend_tile(): value_heads = value_rows.reshape(value_rows.shape[0], head_count, HD)]
    all_to_all x1 -> x0, blocking collectives: 19 us -> none  [on_device(): lax.all_to_all(attended, 'head', split_axis=1, concat_axis=3, tiled=True)]
    reduce_sum x1 -> x0, other arithmetic: 18.3 us -> none  [attend_tile(): weight_sum = jnp.sum(weights, axis=2, keepdims=True)]
    slice x2 -> x0, local copies, waits for them, and re-layouts: 8.21 us -> none  [the longest x1 5.33 us: on_device(): result = attend_tile(query_rows, block[0], block[1], allowed)]
    concatenate x2 -> x0, other arithmetic: 6.82 us -> none  [the longest x1 5.35 us: padded(): jnp.concatenate([lax.ppermute(tail, axis, [(i, (i + 1) % count) for i in...]
  transfers between devices with their start and end apart: 2 -> 0, of which waited for: 2 -> 0; matrix products, arithmetic and copies ran while one was open for 3% -> 0% of each run, Pallas kernels for 0% -> 0%
where the time goes in v1:
time: 117 us
  Pallas kernels  114 us (97%)
  local copies, waits for them, and re-layouts  3.32 us (3%)
    pallas_call x1, Pallas kernels, on_device(): pl.pallas_call(functools.partial(kernel, seq=seq, head=head), out_shape=j...  114 us
    unnamed x1, local copies, waits for them, and re-layouts  3.32 us

profile of v1, /device:TPU:2, one launch (start us, length us, event | category | flops | bytes accessed | tf_op | source)
XLA Modules:
  0.0 117.1 jit_solution(229850979838148361)
XLA Ops:
  0.0 113.7 %tile_attention.1 = bf16[6,64,3072]{2,1,0:T(8,128)(2,1)} custom-call(bf16[768,1536]{1,0:T(8,128)(2,1)} %bitcast.5, bf16[768,1536]{1,0:T(8,128)(2,1)} %bitcast.6, bf16[768,1536]{1,0:T(8,128)(2,1)} %bitcast.7), custom_call_target="tpu_custom_call" | custom-call | flops 10871635968 | bytes 9437184 | tf_op jit(solution)/shard_map/tile_attention/pallas_call | solution.py:192
  113.7 3.3 %copy.5 = bf16[6,8,8,3072]{3,2,1,0:T(8,128)(2,1)} copy(bf16[6,8,8,3072]{3,2,1,0:T(8,128)(2,1)} %bitcast.4) | data formatting | bytes 4718592

commit v2 on v1

--- a/solution.py
+++ b/solution.py
@@ -8,13 +8,14 @@
 from jax.sharding import PartitionSpec as P
 
 HD = 128
-AHEAD = 3
+AHEAD = 4
+RELAY_AHEAD = 2
 MISSING = 1e30
 LOG2E = 1.4426950408889634
 
 
 def kernel(q_ref, k_ref, v_ref, out_ref, q_buf, kv_buf, o_buf,
-           load_sem, send_sem, recv_sem, own_sem, osend_sem, orecv_sem, *, seq, head):
+           load_sem, send_sem, recv_sem, own_sem, osend_sem, orecv_sem, *relay_refs, seq, head):
     heads = q_buf.shape[0]
     tokens = q_buf.shape[1]
     frames = o_buf.shape[1]
@@ -23,6 +24,12 @@
     part = lax.axis_index("head")
     has_left = me > 0
     has_right = me < seq - 1
+    layers = seq // 4
+    layer = me // 4
+    low = me % 4 == 0
+    high = me % 4 == 3
+    if relay_refs:
+        relay_buf, relay_send, relay_recv = relay_refs
 
     def columns(j):
         return pl.ds(pl.multiple_of(j * HD, HD), HD)
@@ -44,6 +51,41 @@
             device_id={"seq": target},
             device_id_type=pl.DeviceIdType.MESH,
         )
+
+    def to_relay(h, side):
+        return pltpu.make_async_remote_copy(
+            src_ref=kv_buf.at[1, h],
+            dst_ref=relay_buf.at[h],
+            send_sem=send_sem.at[side, h],
+            recv_sem=relay_recv.at[h],
+            device_id={"seq": me + 4 if side == 0 else me - 4},
+            device_id_type=pl.DeviceIdType.MESH,
+        )
+
+    def from_relay(h, side):
+        return pltpu.make_async_remote_copy(
+            src_ref=relay_buf.at[h],
+            dst_ref=kv_buf.at[0 if side == 0 else 2, h],
+            send_sem=relay_send.at[h],
+            recv_sem=recv_sem.at[side, h],
+            device_id={"seq": me - 3 if side == 0 else me + 3},
+            device_id_type=pl.DeviceIdType.MESH,
+        )
+
+    def relayed(h, side, at):
+        return h % layers < (at + 1 if side == 0 else layers - at)
+
+    def relays(h, side):
+        if side == 0:
+            return high & (layer > 0) & relayed(h, 0, layer - 1)
+        return low & (layer < layers - 1) & relayed(h, 1, layer + 1)
+
+    def forward(h):
+        for side in range(2):
+            @pl.when(relays(h, side))
+            def _():
+                to_relay(h, side).wait_recv()
+                from_relay(h, side).start()
 
     def out_slices(h, p, sender):
         src = o_buf.at[h, :, pl.ds(pl.multiple_of(p * rows, 16), rows), :]
@@ -74,24 +116,32 @@
     lax.fori_loop(0, heads, start_loads, 0)
 
     barrier = pltpu.get_barrier_semaphore()
-    for near in (lax.rem(me + 1, seq), lax.rem(me + seq - 1, seq)):
+    offsets = (1, seq - 1) + ((3, 4, seq - 3, seq - 4) if relay_refs else ())
+    for offset in offsets:
+        near = lax.rem(me + offset, seq)
         pl.semaphore_signal(barrier, inc=1, device_id={"seq": near}, device_id_type=pl.DeviceIdType.MESH)
     for step in range(1, head):
         pl.semaphore_signal(barrier, inc=1, device_id={"head": lax.rem(part + step, head)},
                             device_id_type=pl.DeviceIdType.MESH)
-    pl.semaphore_wait(barrier, 2 + head - 1)
+    pl.semaphore_wait(barrier, len(offsets) + head - 1)
 
     def send(h):
         for copy in loads(h):
             copy.wait()
 
-        @pl.when(has_right)
-        def _():
-            to_side(h, 0).start()
-
-        @pl.when(has_left)
-        def _():
-            to_side(h, 1).start()
+        for side, exists, edge in ((0, has_right, high), (1, has_left, low)):
+            if relay_refs:
+                by_relay = edge & relayed(h, side, layer)
+
+                @pl.when(exists & by_relay)
+                def _():
+                    to_relay(h, side).start()
+
+                exists = exists & jnp.logical_not(by_relay)
+
+            @pl.when(exists)
+            def _():
+                to_side(h, side).start()
 
     ahead = min(AHEAD, heads)
 
@@ -117,6 +167,14 @@
     chunk = 256 if tokens % 256 == 0 else tokens
     factor = HD ** -0.5 * LOG2E
     per_frame = tokens // frames
+
+    relay_ahead = min(RELAY_AHEAD, heads)
+    if relay_refs:
+        def first_forwards(h, carry):
+            forward(h)
+            return carry
+
+        lax.fori_loop(0, relay_ahead, first_forwards, 0)
 
     def attend(h):
         def rows_of(c, carry):
@@ -148,6 +206,11 @@
         def _():
             send(h + ahead)
 
+        if relay_refs:
+            @pl.when(h + relay_ahead < heads)
+            def _():
+                forward(h + relay_ahead)
+
         @pl.when(has_left)
         def _():
             to_side(h, 0).wait_recv()
@@ -172,6 +235,12 @@
         @pl.when(has_left)
         def _():
             to_side(h, 1).wait_send()
+
+        if relay_refs:
+            for side in range(2):
+                @pl.when(relays(h, side))
+                def _():
+                    from_relay(h, side).wait_send()
 
         to_self(h).wait()
         for step in range(1, head):
@@ -189,6 +258,13 @@
     heads = feat // HD
     tokens = frames * height * width
     rows = height // head * width
+    relay_scratch = []
+    if seq == 16 and head == 2:
+        relay_scratch = [
+            pltpu.VMEM((heads, 2, tokens, HD), jnp.bfloat16),
+            pltpu.SemaphoreType.DMA((heads,)),
+            pltpu.SemaphoreType.DMA((heads,)),
+        ]
     result = pl.pallas_call(
         functools.partial(kernel, seq=seq, head=head),
         out_shape=jax.ShapeDtypeStruct((frames, rows, feat * head), jnp.bfloat16),
@@ -204,7 +280,7 @@
             pltpu.SemaphoreType.DMA((heads,)),
             pltpu.SemaphoreType.DMA((head, heads)),
             pltpu.SemaphoreType.DMA((head, heads)),
-        ],
+        ] + relay_scratch,
         compiler_params=pltpu.CompilerParams(
             collective_id=0, has_side_effects=True, vmem_limit_bytes=56 * 2 ** 20
         ),

time: 117 us -> 120 us (1.026)
  Pallas kernels: 114 us -> 117 us
    pallas_call x1, Pallas kernels: 114 us -> 117 us  [on_device(): pl.pallas_call(functools.partial(kernel, seq=seq, head=head), out_shape=j...]
where the time goes in v2:
time: 120 us
  Pallas kernels  117 us (98%)
  local copies, waits for them, and re-layouts  3.32 us (3%)
    pallas_call x1, Pallas kernels, on_device(): pl.pallas_call(functools.partial(kernel, seq=seq, head=head), out_shape=j...  117 us
    unnamed x1, local copies, waits for them, and re-layouts  3.32 us

profile of v2, /device:TPU:2, one launch (start us, length us, event | category | flops | bytes accessed | tf_op | source)
XLA Modules:
  0.0 120.3 jit_solution(10975767177552841043)
XLA Ops:
  0.0 117.0 %tile_attention.1 = bf16[6,64,3072]{2,1,0:T(8,128)(2,1)} custom-call(bf16[768,1536]{1,0:T(8,128)(2,1)} %bitcast.5, bf16[768,1536]{1,0:T(8,128)(2,1)} %bitcast.6, bf16[768,1536]{1,0:T(8,128)(2,1)} %bitcast.7), custom_call_target="tpu_custom_call" | custom-call | flops 10871635968 | bytes 9437184 | tf_op jit(solution)/shard_map/tile_attention/pallas_call | solution.py:268
  117.0 3.3 %copy.5 = bf16[6,8,8,3072]{3,2,1,0:T(8,128)(2,1)} copy(bf16[6,8,8,3072]{3,2,1,0:T(8,128)(2,1)} %bitcast.4) | data formatting | bytes 4718592

commit v3 on v2

--- a/solution.py
+++ b/solution.py
@@ -58,7 +58,7 @@
             dst_ref=relay_buf.at[h],
             send_sem=send_sem.at[side, h],
             recv_sem=relay_recv.at[h],
-            device_id={"seq": me + 4 if side == 0 else me - 4},
+            device_id={"seq": me - 2 if side == 0 else me + 2},
             device_id_type=pl.DeviceIdType.MESH,
         )
 
@@ -68,17 +68,17 @@
             dst_ref=kv_buf.at[0 if side == 0 else 2, h],
             send_sem=relay_send.at[h],
             recv_sem=recv_sem.at[side, h],
-            device_id={"seq": me - 3 if side == 0 else me + 3},
+            device_id={"seq": me + 3 if side == 0 else me - 3},
             device_id_type=pl.DeviceIdType.MESH,
         )
 
     def relayed(h, side, at):
-        return h % layers < (at + 1 if side == 0 else layers - at)
+        return h % layers < (layers - 1 - at if side == 0 else at)
 
     def relays(h, side):
         if side == 0:
-            return high & (layer > 0) & relayed(h, 0, layer - 1)
-        return low & (layer < layers - 1) & relayed(h, 1, layer + 1)
+            return (me % 4 == 1) & (layer < layers - 1) & relayed(h, 0, layer)
+        return (me % 4 == 2) & (layer > 0) & relayed(h, 1, layer)
 
     def forward(h):
         for side in range(2):
@@ -116,7 +116,7 @@
     lax.fori_loop(0, heads, start_loads, 0)
 
     barrier = pltpu.get_barrier_semaphore()
-    offsets = (1, seq - 1) + ((3, 4, seq - 3, seq - 4) if relay_refs else ())
+    offsets = (1, seq - 1) + ((2, 3, seq - 2, seq - 3) if relay_refs else ())
     for offset in offsets:
         near = lax.rem(me + offset, seq)
         pl.semaphore_signal(barrier, inc=1, device_id={"seq": near}, device_id_type=pl.DeviceIdType.MESH)
@@ -267,9 +267,9 @@
         ]
     result = pl.pallas_call(
         functools.partial(kernel, seq=seq, head=head),
-        out_shape=jax.ShapeDtypeStruct((frames, rows, feat * head), jnp.bfloat16),
+        out_shape=pltpu.VMEM((frames, rows, feat * head), jnp.bfloat16),
         in_specs=[pl.BlockSpec(memory_space=pl.ANY)] * 3,
-        out_specs=pl.BlockSpec(memory_space=pl.ANY),
+        out_specs=pl.BlockSpec(memory_space=pltpu.VMEM),
         scratch_shapes=[
             pltpu.VMEM((heads, tokens, HD), jnp.bfloat16),
             pltpu.VMEM((3, heads, 2, tokens, HD), jnp.bfloat16),

time: 120 us -> 104 us (0.87)
  Pallas kernels: 117 us -> 103 us
  local copies, waits for them, and re-layouts: 3.32 us -> 1.41 us
    pallas_call x1, Pallas kernels: 117 us -> 103 us  [on_device(): pl.pallas_call(functools.partial(kernel, seq=seq, head=head), out_shape=p...]
    unnamed x1, local copies, waits for them, and re-layouts: 3.32 us -> 1.41 us
where the time goes in v3:
time: 104 us
  Pallas kernels  103 us (99%)
  local copies, waits for them, and re-layouts  1.41 us (1%)
    pallas_call x1, Pallas kernels, on_device(): pl.pallas_call(functools.partial(kernel, seq=seq, head=head), out_shape=p...  103 us

profile of v3, /device:TPU:2, one launch (start us, length us, event | category | flops | bytes accessed | tf_op | source)
XLA Modules:
  0.0 104.3 jit_solution(7754009051327356478)
XLA Ops:
  0.0 102.9 %tile_attention.1 = bf16[6,64,3072]{2,1,0:T(8,128)(2,1)S(1)} custom-call(bf16[768,1536]{1,0:T(8,128)(2,1)} %bitcast.5, bf16[768,1536]{1,0:T(8,128)(2,1)} %bitcast.6, bf16[768,1536]{1,0:T(8,128)(2,1)} %bitcast.7), custom_call_target="tpu_custom_call" | custom-call | flops 10871635968 | bytes 9437184 | tf_op jit(solution)/shard_map/tile_attention/pallas_call | solution.py:268
  102.9 1.4 %copy.5 = bf16[6,8,8,3072]{3,2,1,0:T(8,128)(2,1)} copy(bf16[6,8,8,3072]{3,2,1,0:T(8,128)(2,1)S(1)} %bitcast.4) | data formatting | bytes 4718592

commit v4 on v3

--- a/solution.py
+++ b/solution.py
@@ -8,8 +8,9 @@
 from jax.sharding import PartitionSpec as P
 
 HD = 128
-AHEAD = 4
-RELAY_AHEAD = 2
+AHEAD = 3
+RELAY_AHEAD = 1
+LAG = 3
 MISSING = 1e30
 LOG2E = 1.4426950408889634
 
@@ -199,9 +200,36 @@
                 chunk // per_frame, per_frame, HD)
             return carry
 
-        lax.fori_loop(0, tokens // chunk, rows_of, 0)
+        lax.fori_loop(0, tokens // chunk, rows_of, 0, unroll=True)
+
+    lag = min(LAG, heads)
+
+    def finish(h, carry):
+        @pl.when(has_right)
+        def _():
+            to_side(h, 0).wait_send()
+
+        @pl.when(has_left)
+        def _():
+            to_side(h, 1).wait_send()
+
+        if relay_refs:
+            for side in range(2):
+                @pl.when(relays(h, side))
+                def _():
+                    from_relay(h, side).wait_send()
+
+        to_self(h).wait()
+        for step in range(1, head):
+            to_part(h, step).wait_send()
+            to_part(h, step).wait_recv()
+        return carry
 
     def step_of(h, carry):
+        @pl.when(h >= lag)
+        def _():
+            finish(h - lag, 0)
+
         @pl.when(h + ahead < heads)
         def _():
             send(h + ahead)
@@ -227,28 +255,7 @@
 
     lax.fori_loop(0, heads, step_of, 0)
 
-    def finish(h, carry):
-        @pl.when(has_right)
-        def _():
-            to_side(h, 0).wait_send()
-
-        @pl.when(has_left)
-        def _():
-            to_side(h, 1).wait_send()
-
-        if relay_refs:
-            for side in range(2):
-                @pl.when(relays(h, side))
-                def _():
-                    from_relay(h, side).wait_send()
-
-        to_self(h).wait()
-        for step in range(1, head):
-            to_part(h, step).wait_send()
-            to_part(h, step).wait_recv()
-        return carry
-
-    lax.fori_loop(0, heads, finish, 0)
+    lax.fori_loop(heads - lag, heads, finish, 0)
 
 
 def on_device(queries, key_field, value_field):

time: 104 us -> 104 us (level)
  no operation moved by 1% of the time
where the time goes in v4:
time: 104 us
  Pallas kernels  102 us (98%)
  local copies, waits for them, and re-layouts  1.41 us (1%)
    pallas_call x1, Pallas kernels, on_device(): pl.pallas_call(functools.partial(kernel, seq=seq, head=head), out_shape=p...  102 us

profile of v4, /device:TPU:2, one launch (start us, length us, event | category | flops | bytes accessed | tf_op | source)
XLA Modules:
  0.0 103.6 jit_solution(18397177279490687250)
XLA Ops:
  0.0 102.1 %tile_attention.1 = bf16[6,64,3072]{2,1,0:T(8,128)(2,1)S(1)} custom-call(bf16[768,1536]{1,0:T(8,128)(2,1)} %bitcast.5, bf16[768,1536]{1,0:T(8,128)(2,1)} %bitcast.6, bf16[768,1536]{1,0:T(8,128)(2,1)} %bitcast.7), custom_call_target="tpu_custom_call" | custom-call | flops 10871635968 | bytes 9437184 | tf_op jit(solution)/shard_map/tile_attention/pallas_call | solution.py:275
  102.1 1.4 %copy.5 = bf16[6,8,8,3072]{3,2,1,0:T(8,128)(2,1)} copy(bf16[6,8,8,3072]{3,2,1,0:T(8,128)(2,1)S(1)} %bitcast.4) | data formatting | bytes 4718592

commit v5 on v4

--- a/solution.py
+++ b/solution.py
@@ -189,13 +189,13 @@
             tops = [jnp.max(s, axis=1, keepdims=True) - shift[b] for b, s in enumerate(scores)]
             top = jnp.maximum(jnp.maximum(tops[0], tops[1]), tops[2])
             total = 0.0
-            weight_sum = 0.0
+            ones = jnp.ones((tokens, HD), jnp.bfloat16)
             for b in range(3):
                 w = jnp.exp2(scores[b] * factor - (top + shift[b]) * factor)
-                weight_sum = weight_sum + jnp.sum(w, axis=1, keepdims=True)
-                total = total + jnp.dot(w.astype(jnp.bfloat16), kv_buf[b, h, 1],
+                values = jnp.concatenate([kv_buf[b, h, 1], ones], axis=1)
+                total = total + jnp.dot(w.astype(jnp.bfloat16), values,
                                         preferred_element_type=jnp.float32)
-            result = (total / weight_sum).astype(jnp.bfloat16)
+            result = (total[:, :HD] / total[:, HD:]).astype(jnp.bfloat16)
             o_buf[h, pl.ds(c * (chunk // per_frame), chunk // per_frame)] = result.reshape(
                 chunk // per_frame, per_frame, HD)
             return carry

time: 104 us -> 103 us (level)
  no operation moved by 1% of the time
where the time goes in v5:
time: 103 us
  Pallas kernels  102 us (99%)
  local copies, waits for them, and re-layouts  1.41 us (1%)
    pallas_call x1, Pallas kernels, on_device(): pl.pallas_call(functools.partial(kernel, seq=seq, head=head), out_shape=p...  102 us

profile of v5, /device:TPU:2, one launch (start us, length us, event | category | flops | bytes accessed | tf_op | source)
XLA Modules:
  0.0 103.3 jit_solution(1846421160912614391)
XLA Ops:
  0.0 101.9 %tile_attention.1 = bf16[6,64,3072]{2,1,0:T(8,128)(2,1)S(1)} custom-call(bf16[768,1536]{1,0:T(8,128)(2,1)} %bitcast.5, bf16[768,1536]{1,0:T(8,128)(2,1)} %bitcast.6, bf16[768,1536]{1,0:T(8,128)(2,1)} %bitcast.7), custom_call_target="tpu_custom_call" | custom-call | flops 10871635968 | bytes 9437184 | tf_op jit(solution)/shard_map/tile_attention/pallas_call | solution.py:275
  101.9 1.4 %copy.5 = bf16[6,8,8,3072]{3,2,1,0:T(8,128)(2,1)} copy(bf16[6,8,8,3072]{3,2,1,0:T(8,128)(2,1)S(1)} %bitcast.4) | data formatting | bytes 4718592
